TPU v7x, 32 devices: a whole 2x2x4 slice. The times are simulated.
32 devices in a mesh: grp: 1, seq: 8 (over z, y), ch: 4 (over x, core).
Axes of the slice: x: 2, y: 2, z: 4, core: 2. Of those that a mesh axis runs over, the one named last changes fastest.
Arguments:
- inputs: bfloat16 [192, 524288], P('ch', ('grp', 'seq')), may hold values from -6 to 6
- cotangent: bfloat16 [192, 524288], P('ch', ('grp', 'seq')), may hold values from -6 to 6
- kernel: bfloat16 [192, 524288], P('ch', 'seq'), may hold values from 0.25 to 1.75
- right_factor: bfloat16 [1024, 1024], P(('seq', 'ch')), may hold values from -0.1875 to 0.1875
- left_factor: bfloat16 [512, 512], P(('seq', 'ch')), may hold values from -0.25 to 0.25
Outputs:
- mixed_out: bfloat16 [192, 524288], P('ch', ('grp', 'seq'))
- grad_inputs: bfloat16 [192, 524288], P('ch', ('grp', 'seq'))
- grad_kernel: bfloat16 [192, 524288], P('ch', ('grp', 'seq'))
- grad_left: float32 [512, 512], P(('grp', 'seq', 'ch'))
All inputs are finite; a program needn't handle non-finite values.
Results may differ from a plain program's by a relative error of at most 0.0058.
Values may be sent and summed in bfloat16 or wider, within the bound.
A program may use at most 192 MiB of HBM per device.

v0:
```python
import jax
import jax.numpy as jnp
from jax import lax
from jax.sharding import PartitionSpec as P

B1 = 512
B2 = 1024
CH = 192


def shards(inputs, cotangent, kernel, right_factor, left_factor):
    grad_scale = float(CH * B2) ** (-0.5)
    chan_dev = inputs.shape[0]
    seq_count = lax.axis_size("seq")
    loc_rows = B1 // seq_count
    loc_cols = B2 // seq_count
    flat_in = inputs.reshape(chan_dev * loc_rows, B2)
    kern_view = kernel.reshape(chan_dev, loc_rows, B2)
    whole_right = lax.all_gather(right_factor, ("seq", "ch"), axis=0, tiled=True)
    projected = jnp.dot(flat_in, whole_right, preferred_element_type=jnp.float32)
    projected = projected.reshape(chan_dev, loc_rows, B2)
    gated_mix = (projected * kern_view.astype(jnp.float32)).astype(jnp.bfloat16)
    turned = lax.all_to_all(gated_mix, "seq", split_axis=2, concat_axis=1, tiled=True)
    left_whole = lax.all_gather(left_factor, ("seq", "ch"), axis=0, tiled=True)
    mixed = jnp.einsum("pi,cij->cjp", left_whole, turned, preferred_element_type=jnp.float32)
    mixed_out = mixed.astype(jnp.bfloat16).reshape(chan_dev, loc_cols * B1)
    grad_view = cotangent.reshape(chan_dev, loc_cols, B1)
    grad_mix = jnp.einsum(
        "pi,cjp->cij", left_whole, grad_view, preferred_element_type=jnp.float32
    ).astype(jnp.bfloat16)
    left_terms = (
        jnp.einsum("cjp,cij->pi", grad_view, turned, preferred_element_type=jnp.float32)
        * grad_scale
    )
    grad_left = lax.psum_scatter(left_terms, ("seq", "ch"), scatter_dimension=0, tiled=True)
    back_grad = lax.all_to_all(grad_mix, "seq", split_axis=1, concat_axis=2, tiled=True)
    back_wide = back_grad.astype(jnp.float32)
    grad_kernel = (back_wide * projected).astype(jnp.bfloat16).reshape(chan_dev, loc_rows * B2)
    grad_proj = (
        (back_wide * kern_view.astype(jnp.float32))
        .astype(jnp.bfloat16)
        .reshape(chan_dev * loc_rows, B2)
    )
    grad_flat = lax.dot_general(
        grad_proj, whole_right, (((1,), (1,)), ((), ())), preferred_element_type=jnp.float32
    )
    grad_inputs = grad_flat.astype(jnp.bfloat16).reshape(chan_dev, loc_rows * B2)
    return (mixed_out, grad_inputs, grad_kernel, grad_left)


def solution(mesh):
    placed = (
        P("ch", ("grp", "seq")),
        P("ch", ("grp", "seq")),
        P("ch", "seq"),
        P(("seq", "ch"), None),
        P(("seq", "ch"), None),
    )
    return jax.shard_map(
        shards,
        mesh=mesh,
        in_specs=placed,
        out_specs=(
            P("ch", ("grp", "seq")),
            P("ch", ("grp", "seq")),
            P("ch", ("grp", "seq")),
            P(("grp", "seq", "ch"), None),
        ),
        check_vma=False,
    )
```

profile of v0, /device:TPU:0, one launch (start us, length us, event | category | flops | bytes accessed | tf_op | source)
XLA Modules:
  0.0 606.8 jit_solution(14862754045614823590)
XLA Ops:
  7.2 0.0 copy-start.4
  7.2 5.3 copy.49
  12.4 0.0 copy-done.4
  12.4 0.0 copy-start
  12.5 44.6 %all_gather.7 = bf16[512,512]{1,0:T(8,128)(2,1)S(1)} all-gather(bf16[16,512]{1,0:T(8,128)(2,1)S(1)} %copy-done.4), channel_id=1, replica_groups=mesh['grp'=1,'seq'=8,'ch'=4] {'seq','ch'}, dimensions={0}, use_global_device_ids=true | all-gather | bytes 540672 | tf_op jit(solution)/shard_map/all_gather | solution.py:24
  57.1 0.0 copy-start.2
  57.1 0.0 copy-done
  57.1 0.8 copy-done.2
  57.9 5.3 convert_bitcast_fusion.2
  63.2 9.0 %copy.35 = bf16[48,512,128]{2,0,1:T(8,128)(2,1)} copy(bf16[48,512,128]{1,2,0:T(8,128)(2,1)} %convert_bitcast_fusion.2) | data formatting | bytes 12582912 | tf_op jit(solution)/shard_map/convert_element_type | solution.py:30
  72.1 4.8 all-to-all-start.1
  77.0 0.6 all-gather.2.cloned.1.call-start
  77.6 0.2 all-gather.2.cloned.1.call-update
  77.7 0.0 slice-start
  77.7 8.3 %convert_element_type.72 = f32[48,65536]{1,0:T(8,128)} convert(bf16[48,65536]{1,0:T(8,128)(2,1)} %param.7) | non-fusion elementwise | flops 3145728 | bytes 18874368 | tf_op jit(solution)/shard_map/convert_element_type | solution.py:22
  86.0 0.0 slice-start.1
  86.0 16.7 %copy.47 = f32[6,8,64,1024]{3,2,1,0:T(8,128)} copy(f32[6,8,64,1024]{3,1,2,0:T(8,128)} %bitcast.68) | data formatting | bytes 25165824
  102.7 0.0 slice-done
  102.7 0.0 slice-done.1
  102.7 6.6 %copy.46 = bf16[6,8,64,1024]{3,2,1,0:T(8,128)(2,1)} copy(bf16[6,8,64,1024]{3,1,2,0:T(8,128)(2,1)S(1)} %bitcast.76) | data formatting | bytes 12582912
  109.3 110.8 %all-to-all-done.1 = bf16[48,512,128]{2,0,1:T(8,128)(2,1)} async-done(((bf16[48,512,128]{2,0,1:T(8,128)(2,1)}), bf16[48,512,128]{2,0,1:T(8,128)(2,1)}, u32[]{:S(2)}, u32[]{:S(2)}) %all-to-all-start.1) | async-done | bytes 6291488 | tf_op jit(solution)/shard_map/all_to_all | solution.py:36
  220.1 7.1 %copy.36 = bf16[48,512,128]{2,1,0:T(8,128)(2,1)} copy(bf16[48,512,128]{2,0,1:T(8,128)(2,1)} %all-to-all-done.1) | data formatting | bytes 12582912 | tf_op jit(solution)/shard_map/all_to_all | solution.py:36
  227.2 14.6 %convert_bitcast_fusion = (f32[48,8,8,8,128]{4,3,2,1,0:T(8,128)}, f32[48,64,8,128]{3,1,2,0:T(8,128)}) fusion(bf16[48,8,64,128]{3,2,1,0:T(8,128)(2,1)} %bitcast.71), kind=kLoop, calls=%fused_computation | loop fusion | flops 3145728 | bytes 31457280
  241.9 0.0 all-gather.2.cloned.1.call-done
  241.9 17.0 %fusion.2 = (bf16[48,64,1024]{2,1,0:T(8,128)(2,1)}, bf16[48,64,1024]{2,1,0:T(8,128)(2,1)}) fusion(f32[48,8,8,8,128]{4,3,2,1,0:T(8,128)} %get-tuple-element.26, f32[6,8,64,1024]{3,2,1,0:T(8,128)} %copy.47, bf16[48,64,1024]{2,1,0:T(8,128)(2,1)} %bitcast.69, bf16[1024,1024]{1,0:T(8,128)(2,1)} %all-gather.2.cloned.1.call-done), kind=kOutput, calls=%fused_computation.7 | convolution fusion | flops 6455033856 | bytes 46137344 | tf_op jit(solution)/shard_map/dot_general | solution.py:20
  258.9 15.7 %copy.31 = bf16[48,64,1024]{1,0,2:T(8,128)(2,1)} copy(bf16[48,64,1024]{2,1,0:T(8,128)(2,1)} %get-tuple-element.25) | data formatting | bytes 12582912 | tf_op jit(solution)/shard_map/convert_element_type | solution.py:22
  274.6 13.7 %reshape.55 = bf16[8,2,196608]{2,1,0:T(2,128)(2,1)} reshape(bf16[1024,48,64]{2,1,0:T(8,128)(2,1)} %bitcast.66) | data formatting | bytes 12582912
  288.4 4.8 all-to-all-start
  293.1 0.0 reduce-scatter.4.cloned.1.call-start
  293.2 9.1 %reshape.46 = f32[3072,1024]{1,0:T(8,128)} reshape(bf16[48,65536]{1,0:T(8,128)(2,1)} %param.7) | data formatting | bytes 18874368 | tf_op jit(solution)/shard_map/convert_element_type | solution.py:22
  302.3 9.3 %copy.51 = bf16[6,8,64,1024]{3,1,2,0:T(8,128)(2,1)} copy(bf16[6,8,64,1024]{3,2,1,0:T(8,128)(2,1)} %bitcast.70) | data formatting | bytes 12582912
  311.7 21.5 %copy.37 = f32[48,64,8,128]{3,2,1,0:T(8,128)} copy(f32[48,64,8,128]{3,1,2,0:T(8,128)} %get-tuple-element.27) | data formatting | bytes 25165824 | tf_op jit(solution)/shard_map/convert_element_type | solution.py:37
  333.2 98.0 %all-to-all-done = bf16[8,2,196608]{2,1,0:T(2,128)(2,1)} async-done(((bf16[8,2,196608]{2,1,0:T(2,128)(2,1)}), bf16[8,2,196608]{2,1,0:T(2,128)(2,1)}, u32[]{:S(2)}, u32[]{:S(2)}) %all-to-all-start) | async-done | bytes 6291488 | tf_op jit(solution)/shard_map/all_to_all | solution.py:23
  431.2 13.4 %reshape.56 = bf16[1024,48,64]{2,1,0:T(8,128)(2,1)} reshape(bf16[8,2,196608]{2,1,0:T(2,128)(2,1)} %all-to-all-done) | data formatting | bytes 12582912
  444.6 14.1 %copy.33 = bf16[48,8,64,128]{3,2,1,0:T(8,128)(2,1)} copy(bf16[48,8,64,128]{2,0,3,1:T(8,128)(2,1)} %bitcast.67) | data formatting | bytes 12582912 | tf_op jit(solution)/shard_map/all_to_all | solution.py:23
  458.7 0.0 copy-start.1
  458.7 6.7 %fusion.11 = f32[512,512]{0,1:T(8,128)S(1)} fusion(bf16[48,512,128]{2,1,0:T(8,128)(2,1)} %bitcast.82, bf16[48,128,512]{2,1,0:T(8,128)(2,1)} %bitcast.78), kind=kOutput, calls=%fused_computation.16 | convolution fusion | flops 3221487616 | bytes 13631488 | tf_op jit(solution)/shard_map/cjp,cij->pi/dot_general | solution.py:32
  465.4 1.3 copy.43
  466.7 0.0 reduce-scatter.4.cloned.1.call-update
  466.7 0.0 copy-done.1
  466.8 17.8 %fusion.5 = bf16[3072,1024]{1,0:T(8,128)(2,1)} fusion(bf16[1024,1024]{1,0:T(8,128)(2,1)S(1)} %copy-done.1, f32[3072,1024]{1,0:T(8,128)} %reshape.46, f32[384,8,8,128]{3,2,1,0:T(8,128)} %bitcast.72), kind=kOutput, calls=%fused_computation.10 | convolution fusion | flops 6451888128 | bytes 33554432 | tf_op jit(solution)/shard_map/dot_general | solution.py:44
  484.6 0.0 copy-start.3
  484.6 8.1 %reshape.42 = bf16[48,65536]{1,0:T(8,128)(2,1)} reshape(bf16[3072,1024]{1,0:T(8,128)(2,1)} %fusion.5) | data formatting | bytes 12582912 | tf_op jit(solution)/shard_map/reshape | solution.py:47
  492.7 0.0 copy-done.3
  492.7 6.7 %convolution_convert_fusion = bf16[48,128,512]{2,1,0:T(8,128)(2,1)S(1)} fusion(bf16[48,512,128]{2,1,0:T(8,128)(2,1)} %bitcast.83, bf16[512,512]{1,0:T(8,128)(2,1)S(1)} %copy-done.3), kind=kOutput, calls=%fused_computation.11 | convolution fusion | flops 3224371200 | bytes 13107200 | tf_op jit(solution)/shard_map/pi,cij->cjp/dot_general | solution.py:25
  499.5 6.5 %copy.48 = bf16[6,8,128,512]{3,1,2,0:T(8,128)(2,1)} copy(bf16[6,8,128,512]{3,2,1,0:T(8,128)(2,1)S(1)} %bitcast.81) | data formatting | bytes 12582912
  506.0 93.8 %reduce-scatter.4.cloned.1.call-done = f32[16,512]{1,0:T(8,128)} async-done(((f32[512,512]{1,0:T(8,128)}), f32[16,512]{1,0:T(8,128)}) %reduce-scatter.4.cloned.1.call-update) | async-done | bytes 32784
  (1 shorter events, 0.0 us)
Async XLA Ops:
  7.2 5.3 copy-start.4
  12.4 44.7 %copy-start = (bf16[6,8,128,512]{3,2,1,0:T(8,128)(2,1)}, bf16[6,8,128,512]{3,2,1,0:T(8,128)(2,1)S(1)}, u32[]{:S(2)}) copy-start(bf16[6,8,128,512]{3,2,1,0:T(8,128)(2,1)S(1)} %copy.49) | copy-start | bytes 18874372
  57.1 0.8 copy-start.2
  72.1 148.0 %all-to-all-start.1 = ((bf16[48,512,128]{2,0,1:T(8,128)(2,1)}), bf16[48,512,128]{2,0,1:T(8,128)(2,1)}, u32[]{:S(2)}, u32[]{:S(2)}) async-start(bf16[48,512,128]{2,0,1:T(8,128)(2,1)} %copy.35), calls=%async_computation.1 | async-start | bytes 12582912 | tf_op jit(solution)/shard_map/all_to_all | solution.py:36
  77.0 164.9 %all-gather.2.cloned.1.call-start = ((), (), s32[]{:S(2)}) async-start(), calls=%async_computation.3 | async-start | bytes 2162688 | tf_op jit(solution)/shard_map/all_gather | solution.py:19
  77.7 25.0 %slice-start = ((s8[6291456]{0:T(1024)(128)(4,1)}), s8[4194304]{0:T(1024)(128)(4,1)S(1)}, s32[]{:S(2)}) async-start(s8[6291456]{0:T(1024)(128)(4,1)} %bitcast.74), calls=%async_computation.5 | async-start | bytes 8388608
  86.0 16.7 %slice-start.1 = ((s8[6291456]{0:T(1024)(128)(4,1)}), s8[2097152]{0:T(1024)(128)(4,1)S(1)}, s32[]{:S(2)}) async-start(s8[6291456]{0:T(1024)(128)(4,1)} %bitcast.74), calls=%async_computation.6 | async-start | bytes 4194304
  288.4 142.8 %all-to-all-start = ((bf16[8,2,196608]{2,1,0:T(2,128)(2,1)}), bf16[8,2,196608]{2,1,0:T(2,128)(2,1)}, u32[]{:S(2)}, u32[]{:S(2)}) async-start(bf16[8,2,196608]{2,1,0:T(2,128)(2,1)} %reshape.55), calls=%async_computation | async-start | bytes 12582912 | tf_op jit(solution)/shard_map/all_to_all | solution.py:23
  293.1 306.7 %reduce-scatter.4.cloned.1.call-start = ((), (), s32[]{:S(2)}) async-start(), calls=%async_computation.4 | async-start | bytes 1081344
  458.7 8.0 %copy-start.1 = (bf16[1024,1024]{1,0:T(8,128)(2,1)S(1)}, bf16[1024,1024]{1,0:T(8,128)(2,1)}, u32[]{:S(2)}) copy-start(bf16[1024,1024]{1,0:T(8,128)(2,1)} %all-gather.2.cloned.1.call-done) | copy-start | bytes 6291460
  484.6 8.2 %copy-start.3 = (bf16[512,512]{1,0:T(8,128)(2,1)S(1)}, bf16[512,512]{1,0:T(8,128)(2,1)}, u32[]{:S(2)}) copy-start(bf16[512,512]{1,0:T(8,128)(2,1)} %copy-done.2) | copy-start | bytes 1572868
Sparse Core Ops, SparseCore 0:
  80.7 158.2 all-gather.1
  466.9 132.8 reduce-scatter.3
where the time goes:
time: 613 us; the launch traced here: 607 us
  waiting for transfers between devices  303 us (49%)
  local copies, waits for them, and re-layouts  158 us (26%)
  matrix products  53.5 us (9%)
  blocking collectives  44.6 us (7%)
  other arithmetic  22.9 us (4%)
  between operations  14.3 us (2%)
  starting transfers between devices  10.2 us (2%)
    all_to_all x1, waiting for transfers between devices, shards(): lax.all_to_all(grad_mix, 'seq', split_axis=1, concat_axis=2, tiled=True)  111 us
    all_to_all x1, waiting for transfers between devices, shards(): lax.all_to_all(gated_mix, 'seq', split_axis=2, concat_axis=1, tiled=True)  98 us
    unnamed x3, waiting for transfers between devices  94 us
    unnamed x22, local copies, waits for them, and re-layouts  73.7 us
    all_gather x1, blocking collectives, shards(): left_whole = lax.all_gather(left_factor, ('seq', 'ch'), axis=0, tiled=True)  44.6 us
    convert_element_type x2, local copies, waits for them, and re-layouts, shards(): gated_mix = (projected * kern_view.astype(jnp.float32)).astype(jnp.bfloat16)  24.9 us
    convert_element_type x1, local copies, waits for them, and re-layouts, shards(): back_wide = back_grad.astype(jnp.float32)  21.5 us
    dot_general x1, matrix products, shards(): lax.dot_general(grad_proj, whole_right, (((1,), (1,)), ((), ())), preferr...  17.8 us
  transfers between devices with their start and end apart: 4, of which 3 were waited for; matrix products, arithmetic and copies ran while one was open for 22% of the time, Pallas kernels for 0%

commit v1 on v0

--- a/solution.py
+++ b/solution.py
@@ -1,6 +1,10 @@
+import functools
+
 import jax
 import jax.numpy as jnp
 from jax import lax
+from jax.experimental import pallas as pl
+from jax.experimental.pallas import tpu as pltpu
 from jax.sharding import PartitionSpec as P
 
 B1 = 512
@@ -8,7 +12,7 @@
 CH = 192
 
 
-def shards(inputs, cotangent, kernel, right_factor, left_factor):
+def plain_shards(inputs, cotangent, kernel, right_factor, left_factor):
     grad_scale = float(CH * B2) ** (-0.5)
     chan_dev = inputs.shape[0]
     seq_count = lax.axis_size("seq")
@@ -48,6 +52,396 @@
     return (mixed_out, grad_inputs, grad_kernel, grad_left)
 
 
+CHUNK = 16
+LANES = 128
+F32 = jnp.float32
+BF16 = jnp.bfloat16
+MESH = pl.DeviceIdType.MESH
+
+
+def mixer_kernel(
+    seqs, chs, chunks, x_hbm, g_hbm, k_hbm, right_ref, left_ref,
+    mixed_hbm, gin_hbm, gker_hbm, gleft_ref,
+    xbuf, kbuf, out_a, out_b, right_all, left_all, left_turned, turn_i, turn_j,
+    g_rows, a_send, a_recv, d_send, d_recv, gl_turned, gl_sum, gl_ch, gl_mid, gl_seq,
+    io_sem, out_sem, wsend_sem, wrecv_sem, fsend_sem, frecv_sem,
+    asend_sem, arecv_sem, dsend_sem, drecv_sem, csend_sem, crecv_sem, ssend_sem, srecv_sem,
+):
+    me = lax.axis_index("seq")
+    mych = lax.axis_index("ch")
+    rows = B1 // seqs
+    cols = B2 // seqs
+    grad_scale = float(CH * B2) ** (-0.5)
+    wide = CHUNK * cols
+
+    def seq_peer(t):
+        return lax.rem(me + t, seqs)
+
+    def ch_peer(t):
+        return lax.rem(mych + t, chs)
+
+    barrier = pltpu.get_barrier_semaphore()
+
+    def hail_seq(t, _):
+        pl.semaphore_signal(barrier, inc=1, device_id={"seq": seq_peer(t)}, device_id_type=MESH)
+        return 0
+
+    def hail_ch(t, _):
+        pl.semaphore_signal(barrier, inc=1, device_id={"ch": ch_peer(t)}, device_id_type=MESH)
+        return 0
+
+    lax.fori_loop(1, seqs, hail_seq, 0)
+    lax.fori_loop(1, chs, hail_ch, 0)
+
+    def load(src, q, buf, n):
+        return pltpu.make_async_copy(src.at[pl.ds(q * CHUNK, CHUNK), :], buf, io_sem.at[n])
+
+    load(g_hbm, 0, xbuf, 0).start()
+    left_all[me, mych] = left_ref[...]
+    right_all[me, mych] = right_ref[...]
+    pl.semaphore_wait(barrier, seqs + chs - 2)
+
+    def left_seq(frm, to):
+        return pltpu.make_async_remote_copy(
+            left_all.at[frm, mych], left_all.at[frm, mych], wsend_sem.at[0, to],
+            wrecv_sem.at[0, frm], device_id={"seq": to}, device_id_type=MESH)
+
+    def right_seq(frm, to):
+        return pltpu.make_async_remote_copy(
+            right_all.at[frm, mych], right_all.at[frm, mych], wsend_sem.at[1, to],
+            wrecv_sem.at[1, frm], device_id={"seq": to}, device_id_type=MESH)
+
+    def left_ch(frm, to):
+        return pltpu.make_async_remote_copy(
+            left_all.at[:, frm], left_all.at[:, frm], fsend_sem.at[0, to],
+            frecv_sem.at[0, frm], device_id={"ch": to}, device_id_type=MESH)
+
+    def right_ch(frm, to):
+        return pltpu.make_async_remote_copy(
+            right_all.at[:, frm], right_all.at[:, frm], fsend_sem.at[1, to],
+            frecv_sem.at[1, frm], device_id={"ch": to}, device_id_type=MESH)
+
+    def each_seq(f):
+        def step(t, _):
+            f(seq_peer(t))
+            return 0
+        lax.fori_loop(1, seqs, step, 0)
+
+    def each_ch(f):
+        def step(t, _):
+            f(ch_peer(t))
+            return 0
+        lax.fori_loop(1, chs, step, 0)
+
+    each_seq(lambda d: left_seq(me, d).start())
+    each_seq(lambda d: right_seq(me, d).start())
+
+    def turn_grad(q):
+        load(g_hbm, q, xbuf, 0).wait()
+
+        def spread(j, _):
+            for b in range(B1 // LANES):
+                turn_j[b, pl.ds(pl.multiple_of(j * CHUNK, CHUNK), CHUNK), :] = xbuf[
+                    :, pl.ds(pl.multiple_of(j * B1 + b * LANES, LANES), LANES)].astype(F32)
+            return 0
+
+        lax.fori_loop(0, cols, spread, 0, unroll=4)
+
+        def gather(c, _):
+            for b in range(B1 // LANES):
+                g_rows[q, pl.ds(pl.multiple_of(c * cols, cols), cols), b * LANES:(b + 1) * LANES] = turn_j[
+                    b, pl.ds(c, cols, stride=CHUNK), :].astype(BF16)
+            return 0
+
+        lax.fori_loop(0, CHUNK, gather, 0)
+
+    def d_copy(q, frm, to):
+        return pltpu.make_async_remote_copy(
+            d_send.at[q, pl.ds(pl.multiple_of(to * rows, rows), rows), :],
+            d_recv.at[q, pl.ds(pl.multiple_of(frm * rows, rows), rows), :],
+            dsend_sem.at[q, to], drecv_sem.at[q, frm], device_id={"seq": to}, device_id_type=MESH)
+
+    def a_copy(q, frm, to):
+        return pltpu.make_async_remote_copy(
+            a_send.at[q, pl.ds(pl.multiple_of(to * rows, rows), rows), :],
+            a_recv.at[q, pl.ds(pl.multiple_of(frm * rows, rows), rows), :],
+            asend_sem.at[q, to], arecv_sem.at[q, frm], device_id={"seq": to}, device_id_type=MESH)
+
+    def own_copy(send, recv, sem, q):
+        mine = pl.ds(pl.multiple_of(me * rows, rows), rows)
+        return pltpu.make_async_copy(send.at[q, mine, :], recv.at[q, mine, :], sem.at[q, me])
+
+    def make_d(q):
+        def pair(h, _):
+            at = pl.multiple_of(h * 2 * cols, 2 * cols)
+            d_send[q, :, pl.ds(at, 2 * cols)] = lax.dot_general(
+                left_turned[...], g_rows[q, pl.ds(at, 2 * cols), :],
+                (((1,), (1,)), ((), ())), preferred_element_type=F32).astype(BF16)
+            return 0
+
+        lax.fori_loop(0, CHUNK // 2, pair, 0)
+
+    def project(g):
+        lhs = jnp.concatenate(
+            [xbuf[:, pl.ds(pl.multiple_of((g * CHUNK + n) * B2, B2), B2)] for n in range(CHUNK)], axis=0)
+        return jnp.dot(lhs, right_all[...].reshape(B2, B2), preferred_element_type=F32)
+
+    def gates(g):
+        return jnp.concatenate(
+            [kbuf[:, pl.ds(pl.multiple_of((g * CHUNK + n) * B2, B2), B2)] for n in range(CHUNK)], axis=0)
+
+    tall = CHUNK * CHUNK
+
+    def make_a(q):
+        load(x_hbm, q, xbuf, 0).wait()
+        load(k_hbm, q, kbuf, 1).wait()
+
+        def group(g, _):
+            gated = project(g) * gates(g).astype(F32)
+            for d in range(seqs):
+                turn_i[d, pl.ds(pl.multiple_of(g * tall, tall), tall), :] = gated[:, d * cols:(d + 1) * cols]
+            return 0
+
+        lax.fori_loop(0, rows // CHUNK, group, 0)
+
+        def gather(c, _):
+            at = pl.multiple_of(c * cols, cols)
+            for d in range(seqs):
+                a_send[q, d * rows:(d + 1) * rows, pl.ds(at, cols)] = turn_i[
+                    d, pl.ds(c, rows, stride=CHUNK), :].astype(BF16)
+            return 0
+
+        lax.fori_loop(0, CHUNK, gather, 0)
+
+    def send(copy, q, send_buf, recv_buf, sem, earlier):
+        own_copy(send_buf, recv_buf, sem, q).start()
+
+        def one(d):
+            if earlier is not None:
+                earlier[0](earlier[1], me, d).wait_send()
+            copy(q, me, d).start()
+
+        each_seq(one)
+
+    def arrived(copy, q, send_buf, recv_buf, sem):
+        own_copy(send_buf, recv_buf, sem, q).wait()
+        each_seq(lambda d: copy(q, d, me).wait_recv())
+
+    send_d = lambda q, earlier: send(d_copy, q, d_send, d_recv, drecv_sem, earlier)
+    send_a = lambda q, earlier: send(a_copy, q, a_send, a_recv, arecv_sem, earlier)
+
+    def store(buf, dst, q, n):
+        return pltpu.make_async_copy(buf, dst.at[pl.ds(q * CHUNK, CHUNK), :], out_sem.at[n])
+
+    def finish_a(q):
+        arrived(a_copy, q, a_send, a_recv, arecv_sem)
+
+        def pair(h, _):
+            at = pl.multiple_of(h * 2 * cols, 2 * cols)
+            block = a_recv[q, :, pl.ds(at, 2 * cols)]
+            got = jnp.dot(left_all[...].reshape(B1, B1), block, preferred_element_type=F32).T
+            for b in range(B1 // LANES):
+                lanes = slice(b * LANES, (b + 1) * LANES)
+                turn_j[b, pl.ds(2 * h, cols, stride=CHUNK), :] = got[:cols, lanes]
+                turn_j[b, pl.ds(2 * h + 1, cols, stride=CHUNK), :] = got[cols:, lanes]
+            gl_turned[...] += jnp.dot(
+                block, g_rows[q, pl.ds(at, 2 * cols), :], preferred_element_type=F32)
+            return 0
+
+        lax.fori_loop(0, CHUNK // 2, pair, 0)
+
+        def spread(j, _):
+            for b in range(B1 // LANES):
+                out_a[:, pl.ds(pl.multiple_of(j * B1 + b * LANES, LANES), LANES)] = turn_j[
+                    b, pl.ds(pl.multiple_of(j * CHUNK, CHUNK), CHUNK), :].astype(BF16)
+            return 0
+
+        lax.fori_loop(0, cols, spread, 0, unroll=4)
+        store(out_a, mixed_hbm, q, 0).start()
+        store(out_a, mixed_hbm, q, 0).wait()
+
+    def finish_d(q):
+        load(x_hbm, q, xbuf, 0).start()
+        load(k_hbm, q, kbuf, 1).start()
+        load(x_hbm, q, xbuf, 0).wait()
+        load(k_hbm, q, kbuf, 1).wait()
+        arrived(d_copy, q, d_send, d_recv, drecv_sem)
+
+        def gather(c, _):
+            at = pl.multiple_of(c * cols, cols)
+            for s in range(seqs):
+                turn_i[s, pl.ds(c, rows, stride=CHUNK), :] = d_recv[
+                    q, s * rows:(s + 1) * rows, pl.ds(at, cols)].astype(F32)
+            return 0
+
+        lax.fori_loop(0, CHUNK, gather, 0)
+
+        def group(g, _):
+            at = pl.multiple_of(g * tall, tall)
+            back = jnp.concatenate([turn_i[s, pl.ds(at, tall), :] for s in range(seqs)], axis=1)
+            first = (back * project(g)).astype(BF16)
+            for n in range(CHUNK):
+                out_a[:, pl.ds(pl.multiple_of((g * CHUNK + n) * B2, B2), B2)] = first[
+                    n * CHUNK:(n + 1) * CHUNK]
+            inner = (back * gates(g).astype(F32)).astype(BF16)
+            second = lax.dot_general(
+                inner, right_all[...].reshape(B2, B2), (((1,), (1,)), ((), ())),
+                preferred_element_type=F32).astype(BF16)
+            for n in range(CHUNK):
+                out_b[:, pl.ds(pl.multiple_of((g * CHUNK + n) * B2, B2), B2)] = second[
+                    n * CHUNK:(n + 1) * CHUNK]
+            return 0
+
+        lax.fori_loop(0, rows // CHUNK, group, 0)
+        store(out_a, gker_hbm, q, 0).start()
+        store(out_b, gin_hbm, q, 1).start()
+        store(out_a, gker_hbm, q, 0).wait()
+        store(out_b, gin_hbm, q, 1).wait()
+
+    def load_a(q):
+        load(x_hbm, q, xbuf, 0).start()
+        load(k_hbm, q, kbuf, 1).start()
+
+    turn_grad(0)
+    load_a(0)
+    each_seq(lambda d: left_seq(d, me).wait_recv())
+    each_ch(lambda c: left_ch(mych, c).start())
+    each_ch(lambda c: left_ch(c, mych).wait_recv())
+    left_turned[...] = left_all[...].reshape(B1, B1).astype(F32).T.astype(BF16)
+    make_d(0)
+    each_seq(lambda d: right_seq(d, me).wait_recv())
+    each_ch(lambda c: right_ch(mych, c).start())
+    send_d(0, None)
+    each_ch(lambda c: right_ch(c, mych).wait_recv())
+    gl_turned[...] = jnp.zeros_like(gl_turned)
+
+    order = [(d_copy, 0)] + [(a_copy, q) for q in range(chunks)] + [(d_copy, q) for q in range(1, chunks)]
+    make_a(0)
+    send_a(0, None)
+    ready = {("a", 0), ("d", 0)}
+
+    def prepare(kind, q):
+        if (kind, q) in ready:
+            return
+        ready.add((kind, q))
+        if kind == "a":
+            load_a(q)
+            make_a(q)
+        else:
+            load(g_hbm, q, xbuf, 0).start()
+            turn_grad(q)
+            make_d(q)
+
+    for n, (copy, q) in enumerate(order):
+        kind = "a" if copy is a_copy else "d"
+        if n >= 2:
+            prepare(kind, q)
+            (send_a if kind == "a" else send_d)(q, order[n - 2])
+            if n + 1 < len(order):
+                after, qa = order[n + 1]
+                prepare("a" if after is a_copy else "d", qa)
+            was, qw = order[n - 2]
+            if was is a_copy:
+                finish_a(qw)
+            else:
+                finish_d(qw)
+
+    def last(copy, q):
+        if copy is a_copy:
+            finish_a(q)
+        else:
+            finish_d(q)
+
+    def gl_to_ch(frm, to):
+        return pltpu.make_async_remote_copy(
+            gl_sum.at[:, to], gl_ch.at[frm], csend_sem.at[to], crecv_sem.at[frm],
+            device_id={"ch": to}, device_id_type=MESH)
+
+    def gl_to_seq(frm, to):
+        return pltpu.make_async_remote_copy(
+            gl_mid.at[to], gl_seq.at[frm], ssend_sem.at[to], srecv_sem.at[frm],
+            device_id={"seq": to}, device_id_type=MESH)
+
+    gl_sum[...] = (gl_turned[...].T * grad_scale).reshape(gl_sum.shape)
+    each_ch(lambda c: gl_to_ch(mych, c).start())
+    gl_ch[mych] = gl_sum[:, mych]
+    each_ch(lambda c: gl_to_ch(c, mych).wait_recv())
+    total = gl_ch[0]
+    for c in range(1, chs):
+        total = total + gl_ch[c]
+    gl_mid[...] = total
+    each_seq(lambda d: gl_to_seq(me, d).start())
+    gl_seq[me] = gl_mid[me]
+
+    last(*order[-2])
+    each_seq(lambda d: gl_to_seq(d, me).wait_recv())
+    whole = gl_seq[0]
+    for s in range(1, seqs):
+        whole = whole + gl_seq[s]
+    gleft_ref[...] = whole
+    last(*order[-1])
+
+    for copy, q in order[-2:]:
+        each_seq(lambda d: copy(q, me, d).wait_send())
+    each_seq(lambda d: left_seq(me, d).wait_send())
+    each_seq(lambda d: right_seq(me, d).wait_send())
+    each_ch(lambda c: left_ch(mych, c).wait_send())
+    each_ch(lambda c: right_ch(mych, c).wait_send())
+    each_ch(lambda c: gl_to_ch(mych, c).wait_send())
+    each_seq(lambda d: gl_to_seq(me, d).wait_send())
+
+
+def shards(inputs, cotangent, kernel, right_factor, left_factor):
+    seqs, chs = lax.axis_size("seq"), lax.axis_size("ch")
+    chan_dev, span = inputs.shape
+    rows, cols = B1 // seqs, B2 // seqs
+    if chan_dev % CHUNK or cols != LANES or rows % CHUNK or chan_dev < 3 * CHUNK:
+        return plain_shards(inputs, cotangent, kernel, right_factor, left_factor)
+    chunks = chan_dev // CHUNK
+    wide = CHUNK * cols
+    any_spec = pl.BlockSpec(memory_space=pl.ANY)
+    vmem_spec = pl.BlockSpec(memory_space=pltpu.VMEM)
+    dma = pltpu.SemaphoreType.DMA
+    big = jax.ShapeDtypeStruct((chan_dev, span), BF16)
+    part = B1 // (seqs * chs)
+    flops = 2 * chan_dev * B1 * B2 * (3 * B2 + 3 * B1) // seqs
+    return pl.pallas_call(
+        functools.partial(mixer_kernel, seqs, chs, chunks),
+        out_shape=(big, big, big, jax.ShapeDtypeStruct((part, B1), F32)),
+        in_specs=[any_spec] * 3 + [vmem_spec] * 2,
+        out_specs=(any_spec, any_spec, any_spec, vmem_spec),
+        scratch_shapes=[
+            pltpu.VMEM((CHUNK, span), BF16),
+            pltpu.VMEM((CHUNK, span), BF16),
+            pltpu.VMEM((CHUNK, span), BF16),
+            pltpu.VMEM((CHUNK, span), BF16),
+            pltpu.VMEM((seqs, chs, B2 // (seqs * chs), B2), BF16),
+            pltpu.VMEM((seqs, chs, part, B1), BF16),
+            pltpu.VMEM((B1, B1), BF16),
+            pltpu.VMEM((seqs, CHUNK * rows, cols), F32),
+            pltpu.VMEM((B1 // LANES, CHUNK * cols, LANES), F32),
+            pltpu.VMEM((chunks, wide, B1), BF16),
+            pltpu.VMEM((chunks, B1, wide), BF16),
+            pltpu.VMEM((chunks, B1, wide), BF16),
+            pltpu.VMEM((chunks, B1, wide), BF16),
+            pltpu.VMEM((chunks, B1, wide), BF16),
+            pltpu.VMEM((B1, B1), F32),
+            pltpu.VMEM((seqs, chs, part, B1), F32),
+            pltpu.VMEM((chs, seqs, part, B1), F32),
+            pltpu.VMEM((seqs, part, B1), F32),
+            pltpu.VMEM((seqs, part, B1), F32),
+            dma((2,)), dma((2,)),
+            dma((2, seqs)), dma((2, seqs)), dma((2, chs)), dma((2, chs)),
+            dma((chunks, seqs)), dma((chunks, seqs)), dma((chunks, seqs)), dma((chunks, seqs)),
+            dma((chs,)), dma((chs,)), dma((seqs,)), dma((seqs,)),
+        ],
+        compiler_params=pltpu.CompilerParams(
+            collective_id=0, has_side_effects=True, vmem_limit_bytes=62 * 1024 * 1024),
+        cost_estimate=pl.CostEstimate(flops=flops, bytes_accessed=12 * chan_dev * span, transcendentals=0),
+        name="monarch_mixer",
+    )(inputs, cotangent, kernel, right_factor, left_factor)
+
+
 def solution(mesh):
     placed = (
         P("ch", ("grp", "seq")),

time: 613 us -> 335 us (0.55)
  the two profiles are of different devices: /device:TPU:0 before, /device:TPU:31 now
where the time goes in v1:
time: 335 us
  Pallas kernels  320 us (96%)
  local copies, waits for them, and re-layouts  14.4 us (4%)
    pallas_call x1, Pallas kernels, shards(): pl.pallas_call(functools.partial(mixer_kernel, seqs, chs, chunks), out_sh...  320 us
    unnamed x12, local copies, waits for them, and re-layouts  14.4 us

profile of v1, /device:TPU:31, one launch (start us, length us, event | category | flops | bytes accessed | tf_op | source)
XLA Modules:
  0.0 334.7 jit_solution(14777983650665605783)
XLA Ops:
  0.6 319.6 %monarch_mixer.1 = (bf16[48,65536]{1,0:T(8,128)(2,1)}, bf16[48,65536]{1,0:T(8,128)(2,1)}, bf16[48,65536]{1,0:T(8,128)(2,1)}, f32[16,512]{1,0:T(8,128)}) custom-call(bf16[48,65536]{1,0:T(8,128)(2,1)} %x_hbm.1, bf16[48,65536]{1,0:T(8,128)(2,1)} %g_hbm.1, bf16[48,65536]{1,0:T(8,128)(2,1)} %k_hbm.1, bf16[32,1024]{1,0:T(8,128)(2,1)} %right_ref.1, ...), custom_call_target="tpu_custom_call" | custom-call | flops 28991029248 | bytes 37748736 | tf_op jit(solution)/shard_map/monarch_mixer/pallas_call | solution.py:408
  320.2 0.0 copy-start
  320.2 0.0 slice-start
  320.2 6.5 %copy.13 = bf16[48,65536]{1,0:T(8,128)(2,1)} copy(bf16[48,65536]{1,0:T(8,128)(2,1)} %get-tuple-element.8) | data formatting | bytes 12582912
  326.8 0.0 copy-done
  326.8 0.0 slice-start.1
  326.8 3.2 copy.14
  330.0 0.0 slice-done
  330.0 1.4 slice-done.1
  331.3 0.0 copy-start.1
  331.3 2.7 copy.15
  334.0 0.0 copy-done.1
  334.1 0.6 copy.16
  (1 shorter events, 0.0 us)
Async XLA Ops:
  320.2 6.6 %copy-start = (bf16[48,65536]{1,0:T(8,128)(2,1)S(1)}, bf16[48,65536]{1,0:T(8,128)(2,1)}, u32[]{:S(2)}) copy-start(bf16[48,65536]{1,0:T(8,128)(2,1)} %get-tuple-element.9) | copy-start | bytes 18874372
  320.2 9.7 %slice-start = ((s8[6291456]{0:T(1024)(128)(4,1)}), s8[4194304]{0:T(1024)(128)(4,1)S(1)}, s32[]{:S(2)}) async-start(s8[6291456]{0:T(1024)(128)(4,1)} %bitcast), calls=%async_computation | async-start | bytes 8388608
  326.8 4.6 %slice-start.1 = ((s8[6291456]{0:T(1024)(128)(4,1)}), s8[2097152]{0:T(1024)(128)(4,1)S(1)}, s32[]{:S(2)}) async-start(s8[6291456]{0:T(1024)(128)(4,1)} %bitcast), calls=%async_computation.1 | async-start | bytes 4194304
  331.3 2.7 copy-start.1

commit v2 on v1

--- a/solution.py
+++ b/solution.py
@@ -63,9 +63,10 @@
     seqs, chs, chunks, x_hbm, g_hbm, k_hbm, right_ref, left_ref,
     mixed_hbm, gin_hbm, gker_hbm, gleft_ref,
     xbuf, kbuf, out_a, out_b, right_all, left_all, left_turned, turn_i, turn_j,
-    g_rows, a_send, a_recv, d_send, d_recv, gl_turned, gl_sum, gl_ch, gl_mid, gl_seq,
+    g_rows, a_send, a_recv, d_send, d_recv, gl_turned, gl_sum, gl_ch, gl_mid, gl_side, gl_stand,
     io_sem, out_sem, wsend_sem, wrecv_sem, fsend_sem, frecv_sem,
     asend_sem, arecv_sem, dsend_sem, drecv_sem, csend_sem, crecv_sem, ssend_sem, srecv_sem,
+    own_sem, part_sem,
 ):
     me = lax.axis_index("seq")
     mych = lax.axis_index("ch")
@@ -77,6 +78,14 @@
     def seq_peer(t):
         return lax.rem(me + t, seqs)
 
+    def flip(mask):
+        place, bit = 0, 1
+        while bit < seqs:
+            digit = lax.rem(lax.div(me, bit), 2)
+            place = place + bit * (1 - digit if mask & bit else digit)
+            bit *= 2
+        return place
+
     def ch_peer(t):
         return lax.rem(mych + t, chs)
 
@@ -106,10 +115,26 @@
             left_all.at[frm, mych], left_all.at[frm, mych], wsend_sem.at[0, to],
             wrecv_sem.at[0, frm], device_id={"seq": to}, device_id_type=MESH)
 
-    def right_seq(frm, to):
-        return pltpu.make_async_remote_copy(
-            right_all.at[frm, mych], right_all.at[frm, mych], wsend_sem.at[1, to],
-            wrecv_sem.at[1, frm], device_id={"seq": to}, device_id_type=MESH)
+    hops, held, number = [], [0], 0
+    bit = seqs // 2
+    while bit:
+        hops.append([(number + n, mask, bit) for n, mask in enumerate(held)])
+        number += len(held)
+        held = held + [mask + bit for mask in held]
+        bit //= 2
+
+    def right_seq(n, block, to):
+        return pltpu.make_async_remote_copy(
+            right_all.at[block, mych], right_all.at[block, mych], wsend_sem.at[1, n],
+            wrecv_sem.at[1, block], device_id={"seq": to}, device_id_type=MESH)
+
+    def right_hop(h):
+        for n, mask, to in hops[h]:
+            right_seq(n, flip(mask), flip(to)).start()
+
+    def right_hop_done(h):
+        for n, mask, to in hops[h]:
+            right_seq(n, flip(mask + to), me).wait_recv()
 
     def left_ch(frm, to):
         return pltpu.make_async_remote_copy(
@@ -134,7 +159,7 @@
         lax.fori_loop(1, chs, step, 0)
 
     each_seq(lambda d: left_seq(me, d).start())
-    each_seq(lambda d: right_seq(me, d).start())
+    right_hop(0)
 
     def turn_grad(q):
         load(g_hbm, q, xbuf, 0).wait()
@@ -155,11 +180,14 @@
 
         lax.fori_loop(0, CHUNK, gather, 0)
 
-    def d_copy(q, frm, to):
-        return pltpu.make_async_remote_copy(
-            d_send.at[q, pl.ds(pl.multiple_of(to * rows, rows), rows), :],
-            d_recv.at[q, pl.ds(pl.multiple_of(frm * rows, rows), rows), :],
-            dsend_sem.at[q, to], drecv_sem.at[q, frm], device_id={"seq": to}, device_id_type=MESH)
+    pieces = rows // CHUNK
+
+    def d_copy(q, g, frm, to):
+        return pltpu.make_async_remote_copy(
+            d_send.at[q, pl.ds(pl.multiple_of(to * rows + g * CHUNK, CHUNK), CHUNK), :],
+            d_recv.at[q, pl.ds(pl.multiple_of(frm * rows + g * CHUNK, CHUNK), CHUNK), :],
+            dsend_sem.at[q, g, to], drecv_sem.at[q, g, frm],
+            device_id={"seq": to}, device_id_type=MESH)
 
     def a_copy(q, frm, to):
         return pltpu.make_async_remote_copy(
@@ -167,9 +195,9 @@
             a_recv.at[q, pl.ds(pl.multiple_of(frm * rows, rows), rows), :],
             asend_sem.at[q, to], arecv_sem.at[q, frm], device_id={"seq": to}, device_id_type=MESH)
 
-    def own_copy(send, recv, sem, q):
+    def own_copy(send, recv, q, n):
         mine = pl.ds(pl.multiple_of(me * rows, rows), rows)
-        return pltpu.make_async_copy(send.at[q, mine, :], recv.at[q, mine, :], sem.at[q, me])
+        return pltpu.make_async_copy(send.at[q, mine, :], recv.at[q, mine, :], own_sem.at[n, q])
 
     def make_d(q):
         def pair(h, _):
@@ -213,28 +241,45 @@
 
         lax.fori_loop(0, CHUNK, gather, 0)
 
-    def send(copy, q, send_buf, recv_buf, sem, earlier):
-        own_copy(send_buf, recv_buf, sem, q).start()
+    def sent(kind, q, d):
+        if kind == "a":
+            a_copy(q, me, d).wait_send()
+        else:
+            for g in range(pieces):
+                d_copy(q, g, me, d).wait_send()
+
+    def send_a(q, earlier):
+        own_copy(a_send, a_recv, q, 0).start()
 
         def one(d):
             if earlier is not None:
-                earlier[0](earlier[1], me, d).wait_send()
-            copy(q, me, d).start()
+                sent(*earlier, d)
+            a_copy(q, me, d).start()
 
         each_seq(one)
 
-    def arrived(copy, q, send_buf, recv_buf, sem):
-        own_copy(send_buf, recv_buf, sem, q).wait()
-        each_seq(lambda d: copy(q, d, me).wait_recv())
-
-    send_d = lambda q, earlier: send(d_copy, q, d_send, d_recv, drecv_sem, earlier)
-    send_a = lambda q, earlier: send(a_copy, q, a_send, a_recv, arecv_sem, earlier)
+    def send_d(q, earlier):
+        own_copy(d_send, d_recv, q, 1).start()
+
+        def first(d):
+            if earlier is not None:
+                sent(*earlier, d)
+            d_copy(q, 0, me, d).start()
+
+        each_seq(first)
+
+        def later(g, _):
+            each_seq(lambda d: d_copy(q, g, me, d).start())
+            return 0
+
+        lax.fori_loop(1, pieces, later, 0)
 
     def store(buf, dst, q, n):
         return pltpu.make_async_copy(buf, dst.at[pl.ds(q * CHUNK, CHUNK), :], out_sem.at[n])
 
     def finish_a(q):
-        arrived(a_copy, q, a_send, a_recv, arecv_sem)
+        own_copy(a_send, a_recv, q, 0).wait()
+        each_seq(lambda d: a_copy(q, d, me).wait_recv())
 
         def pair(h, _):
             at = pl.multiple_of(h * 2 * cols, 2 * cols)
@@ -265,24 +310,26 @@
         load(k_hbm, q, kbuf, 1).start()
         load(x_hbm, q, xbuf, 0).wait()
         load(k_hbm, q, kbuf, 1).wait()
-        arrived(d_copy, q, d_send, d_recv, drecv_sem)
-
-        def gather(c, _):
-            at = pl.multiple_of(c * cols, cols)
-            for s in range(seqs):
-                turn_i[s, pl.ds(c, rows, stride=CHUNK), :] = d_recv[
-                    q, s * rows:(s + 1) * rows, pl.ds(at, cols)].astype(F32)
-            return 0
-
-        lax.fori_loop(0, CHUNK, gather, 0)
+        own_copy(d_send, d_recv, q, 1).wait()
+
+        def part(buf, dst, g, n):
+            span = pl.ds(pl.multiple_of(g * CHUNK * B2, CHUNK * B2), CHUNK * B2)
+            return pltpu.make_async_copy(
+                buf.at[:, span], dst.at[pl.ds(q * CHUNK, CHUNK), span], part_sem.at[n, g])
 
         def group(g, _):
+            each_seq(lambda d: d_copy(q, g, d, me).wait_recv())
             at = pl.multiple_of(g * tall, tall)
+
+            def gather(c, _):
+                lanes = pl.ds(pl.multiple_of(c * cols, cols), cols)
+                for s in range(seqs):
+                    turn_i[s, pl.ds(at + c, CHUNK, stride=CHUNK), :] = d_recv[
+                        q, pl.ds(pl.multiple_of(s * rows + g * CHUNK, CHUNK), CHUNK), lanes].astype(F32)
+                return 0
+
+            lax.fori_loop(0, CHUNK, gather, 0, unroll=4)
             back = jnp.concatenate([turn_i[s, pl.ds(at, tall), :] for s in range(seqs)], axis=1)
-            first = (back * project(g)).astype(BF16)
-            for n in range(CHUNK):
-                out_a[:, pl.ds(pl.multiple_of((g * CHUNK + n) * B2, B2), B2)] = first[
-                    n * CHUNK:(n + 1) * CHUNK]
             inner = (back * gates(g).astype(F32)).astype(BF16)
             second = lax.dot_general(
                 inner, right_all[...].reshape(B2, B2), (((1,), (1,)), ((), ())),
@@ -290,13 +337,22 @@
             for n in range(CHUNK):
                 out_b[:, pl.ds(pl.multiple_of((g * CHUNK + n) * B2, B2), B2)] = second[
                     n * CHUNK:(n + 1) * CHUNK]
-            return 0
-
-        lax.fori_loop(0, rows // CHUNK, group, 0)
-        store(out_a, gker_hbm, q, 0).start()
-        store(out_b, gin_hbm, q, 1).start()
-        store(out_a, gker_hbm, q, 0).wait()
-        store(out_b, gin_hbm, q, 1).wait()
+            part(out_b, gin_hbm, g, 1).start()
+            first = (back * project(g)).astype(BF16)
+            for n in range(CHUNK):
+                out_a[:, pl.ds(pl.multiple_of((g * CHUNK + n) * B2, B2), B2)] = first[
+                    n * CHUNK:(n + 1) * CHUNK]
+            part(out_a, gker_hbm, g, 0).start()
+            return 0
+
+        lax.fori_loop(0, pieces, group, 0)
+
+        def written(g, _):
+            part(out_a, gker_hbm, g, 0).wait()
+            part(out_b, gin_hbm, g, 1).wait()
+            return 0
+
+        lax.fori_loop(0, pieces, written, 0)
 
     def load_a(q):
         load(x_hbm, q, xbuf, 0).start()
@@ -307,15 +363,20 @@
     each_seq(lambda d: left_seq(d, me).wait_recv())
     each_ch(lambda c: left_ch(mych, c).start())
     each_ch(lambda c: left_ch(c, mych).wait_recv())
+    for h in range(1, len(hops) - 1):
+        right_hop_done(h - 1)
+        right_hop(h)
     left_turned[...] = left_all[...].reshape(B1, B1).astype(F32).T.astype(BF16)
     make_d(0)
-    each_seq(lambda d: right_seq(d, me).wait_recv())
+    right_hop_done(len(hops) - 2)
+    right_hop(len(hops) - 1)
+    send_d(0, None)
+    right_hop_done(len(hops) - 1)
     each_ch(lambda c: right_ch(mych, c).start())
-    send_d(0, None)
     each_ch(lambda c: right_ch(c, mych).wait_recv())
     gl_turned[...] = jnp.zeros_like(gl_turned)
 
-    order = [(d_copy, 0)] + [(a_copy, q) for q in range(chunks)] + [(d_copy, q) for q in range(1, chunks)]
+    order = [("d", 0)] + [("a", q) for q in range(chunks)] + [("d", q) for q in range(1, chunks)]
     make_a(0)
     send_a(0, None)
     ready = {("a", 0), ("d", 0)}
@@ -332,35 +393,43 @@
             turn_grad(q)
             make_d(q)
 
-    for n, (copy, q) in enumerate(order):
-        kind = "a" if copy is a_copy else "d"
+    def finish(kind, q):
+        if kind == "a":
+            finish_a(q)
+        else:
+            finish_d(q)
+
+    for n, (kind, q) in enumerate(order):
         if n >= 2:
             prepare(kind, q)
             (send_a if kind == "a" else send_d)(q, order[n - 2])
             if n + 1 < len(order):
-                after, qa = order[n + 1]
-                prepare("a" if after is a_copy else "d", qa)
-            was, qw = order[n - 2]
-            if was is a_copy:
-                finish_a(qw)
-            else:
-                finish_d(qw)
-
-    def last(copy, q):
-        if copy is a_copy:
-            finish_a(q)
-        else:
-            finish_d(q)
+                prepare(*order[n + 1])
+            finish(*order[n - 2])
 
     def gl_to_ch(frm, to):
         return pltpu.make_async_remote_copy(
             gl_sum.at[:, to], gl_ch.at[frm], csend_sem.at[to], crecv_sem.at[frm],
             device_id={"ch": to}, device_id_type=MESH)
 
-    def gl_to_seq(frm, to):
-        return pltpu.make_async_remote_copy(
-            gl_mid.at[to], gl_seq.at[frm], ssend_sem.at[to], srecv_sem.at[frm],
-            device_id={"seq": to}, device_id_type=MESH)
+    side = lax.rem(me, 2)
+    stand = lax.div(me, 2)
+
+    def gl_to_side(frm, to):
+        return pltpu.make_async_remote_copy(
+            gl_mid.at[:, to], gl_side, ssend_sem.at[seqs - 1], srecv_sem.at[seqs - 1],
+            device_id={"seq": flip(1)}, device_id_type=MESH)
+
+    def gl_to_stand(frm, to):
+        return pltpu.make_async_remote_copy(
+            gl_side.at[to], gl_stand.at[frm], ssend_sem.at[to], srecv_sem.at[frm],
+            device_id={"seq": to * 2 + side}, device_id_type=MESH)
+
+    def each_stand(f):
+        def step(t, _):
+            f(lax.rem(stand + t, seqs // 2))
+            return 0
+        lax.fori_loop(1, seqs // 2, step, 0)
 
     gl_sum[...] = (gl_turned[...].T * grad_scale).reshape(gl_sum.shape)
     each_ch(lambda c: gl_to_ch(mych, c).start())
@@ -369,33 +438,39 @@
     total = gl_ch[0]
     for c in range(1, chs):
         total = total + gl_ch[c]
-    gl_mid[...] = total
-    each_seq(lambda d: gl_to_seq(me, d).start())
-    gl_seq[me] = gl_mid[me]
-
-    last(*order[-2])
-    each_seq(lambda d: gl_to_seq(d, me).wait_recv())
-    whole = gl_seq[0]
-    for s in range(1, seqs):
-        whole = whole + gl_seq[s]
+    gl_mid[...] = total.reshape(gl_mid.shape)
+    gl_to_side(side, 1 - side).start()
+    gl_to_side(1 - side, side).wait_recv()
+    gl_side[...] += gl_mid[:, side]
+    each_stand(lambda z: gl_to_stand(stand, z).start())
+    gl_stand[stand] = gl_side[stand]
+
+    finish(*order[-2])
+    each_stand(lambda z: gl_to_stand(z, stand).wait_recv())
+    whole = gl_stand[0]
+    for z in range(1, seqs // 2):
+        whole = whole + gl_stand[z]
     gleft_ref[...] = whole
-    last(*order[-1])
-
-    for copy, q in order[-2:]:
-        each_seq(lambda d: copy(q, me, d).wait_send())
+    finish(*order[-1])
+
+    for kind, q in order[-2:]:
+        each_seq(lambda d: sent(kind, q, d))
     each_seq(lambda d: left_seq(me, d).wait_send())
-    each_seq(lambda d: right_seq(me, d).wait_send())
+    for hop in hops:
+        for n, mask, to in hop:
+            right_seq(n, flip(mask), flip(to)).wait_send()
     each_ch(lambda c: left_ch(mych, c).wait_send())
     each_ch(lambda c: right_ch(mych, c).wait_send())
     each_ch(lambda c: gl_to_ch(mych, c).wait_send())
-    each_seq(lambda d: gl_to_seq(me, d).wait_send())
+    gl_to_side(side, 1 - side).wait_send()
+    each_stand(lambda z: gl_to_stand(stand, z).wait_send())
 
 
 def shards(inputs, cotangent, kernel, right_factor, left_factor):
     seqs, chs = lax.axis_size("seq"), lax.axis_size("ch")
     chan_dev, span = inputs.shape
     rows, cols = B1 // seqs, B2 // seqs
-    if chan_dev % CHUNK or cols != LANES or rows % CHUNK or chan_dev < 3 * CHUNK:
+    if chan_dev % CHUNK or cols != LANES or seqs & (seqs - 1) or seqs < 4 or rows % CHUNK or chan_dev < 3 * CHUNK:
         return plain_shards(inputs, cotangent, kernel, right_factor, left_factor)
     chunks = chan_dev // CHUNK
     wide = CHUNK * cols
@@ -428,12 +503,15 @@
             pltpu.VMEM((B1, B1), F32),
             pltpu.VMEM((seqs, chs, part, B1), F32),
             pltpu.VMEM((chs, seqs, part, B1), F32),
-            pltpu.VMEM((seqs, part, B1), F32),
-            pltpu.VMEM((seqs, part, B1), F32),
-            dma((2,)), dma((2,)),
+            pltpu.VMEM((seqs // 2, 2, part, B1), F32),
+            pltpu.VMEM((seqs // 2, part, B1), F32),
+            pltpu.VMEM((seqs // 2, part, B1), F32),
+            dma((2,)), dma((1,)),
             dma((2, seqs)), dma((2, seqs)), dma((2, chs)), dma((2, chs)),
-            dma((chunks, seqs)), dma((chunks, seqs)), dma((chunks, seqs)), dma((chunks, seqs)),
+            dma((chunks, seqs)), dma((chunks, seqs)),
+            dma((chunks, rows // CHUNK, seqs)), dma((chunks, rows // CHUNK, seqs)),
             dma((chs,)), dma((chs,)), dma((seqs,)), dma((seqs,)),
+            dma((2, chunks)), dma((2, rows // CHUNK)),
         ],
         compiler_params=pltpu.CompilerParams(
             collective_id=0, has_side_effects=True, vmem_limit_bytes=62 * 1024 * 1024),

time: 335 us -> 328 us (0.979)
  the two profiles are of different devices: /device:TPU:31 before, /device:TPU:0 now
where the time goes in v2:
time: 328 us
  Pallas kernels  313 us (95%)
  local copies, waits for them, and re-layouts  14.4 us (4%)
    pallas_call x1, Pallas kernels, shards(): pl.pallas_call(functools.partial(mixer_kernel, seqs, chs, chunks), out_sh...  313 us
    unnamed x12, local copies, waits for them, and re-layouts  14.4 us

profile of v2, /device:TPU:0, one launch (start us, length us, event | category | flops | bytes accessed | tf_op | source)
XLA Modules:
  0.0 327.8 jit_solution(17493141234676810682)
XLA Ops:
  0.6 312.7 %monarch_mixer.1 = (bf16[48,65536]{1,0:T(8,128)(2,1)}, bf16[48,65536]{1,0:T(8,128)(2,1)}, bf16[48,65536]{1,0:T(8,128)(2,1)}, f32[16,512]{1,0:T(8,128)}) custom-call(bf16[48,65536]{1,0:T(8,128)(2,1)} %x_hbm.1, bf16[48,65536]{1,0:T(8,128)(2,1)} %g_hbm.1, bf16[48,65536]{1,0:T(8,128)(2,1)} %k_hbm.1, bf16[32,1024]{1,0:T(8,128)(2,1)} %right_ref.1, ...), custom_call_target="tpu_custom_call" | custom-call | flops 28991029248 | bytes 37748736 | tf_op jit(solution)/shard_map/monarch_mixer/pallas_call | solution.py:483
  313.3 0.0 copy-start
  313.3 0.0 slice-start
  313.3 6.5 %copy.13 = bf16[48,65536]{1,0:T(8,128)(2,1)} copy(bf16[48,65536]{1,0:T(8,128)(2,1)} %get-tuple-element.8) | data formatting | bytes 12582912
  319.9 0.0 copy-done
  319.9 0.0 slice-start.1
  319.9 3.2 copy.14
  323.1 0.0 slice-done
  323.1 1.4 slice-done.1
  324.4 0.0 copy-start.1
  324.4 2.7 copy.15
  327.1 0.0 copy-done.1
  327.1 0.6 copy.16
  (1 shorter events, 0.0 us)
Async XLA Ops:
  313.3 6.6 %copy-start = (bf16[48,65536]{1,0:T(8,128)(2,1)S(1)}, bf16[48,65536]{1,0:T(8,128)(2,1)}, u32[]{:S(2)}) copy-start(bf16[48,65536]{1,0:T(8,128)(2,1)} %get-tuple-element.9) | copy-start | bytes 18874372
  313.3 9.7 %slice-start = ((s8[6291456]{0:T(1024)(128)(4,1)}), s8[4194304]{0:T(1024)(128)(4,1)S(1)}, s32[]{:S(2)}) async-start(s8[6291456]{0:T(1024)(128)(4,1)} %bitcast), calls=%async_computation | async-start | bytes 8388608
  319.9 4.6 %slice-start.1 = ((s8[6291456]{0:T(1024)(128)(4,1)}), s8[2097152]{0:T(1024)(128)(4,1)S(1)}, s32[]{:S(2)}) async-start(s8[6291456]{0:T(1024)(128)(4,1)} %bitcast), calls=%async_computation.1 | async-start | bytes 4194304
  324.4 2.7 copy-start.1

commit v3 on v2

--- a/solution.py
+++ b/solution.py
@@ -362,14 +362,14 @@
     load_a(0)
     each_seq(lambda d: left_seq(d, me).wait_recv())
     each_ch(lambda c: left_ch(mych, c).start())
-    each_ch(lambda c: left_ch(c, mych).wait_recv())
     for h in range(1, len(hops) - 1):
         right_hop_done(h - 1)
         right_hop(h)
+    each_ch(lambda c: left_ch(c, mych).wait_recv())
     left_turned[...] = left_all[...].reshape(B1, B1).astype(F32).T.astype(BF16)
-    make_d(0)
     right_hop_done(len(hops) - 2)
     right_hop(len(hops) - 1)
+    make_d(0)
     send_d(0, None)
     right_hop_done(len(hops) - 1)
     each_ch(lambda c: right_ch(mych, c).start())

time: 328 us -> 326 us (level)
  no operation moved by 1% of the time
where the time goes in v3:
time: 326 us
  Pallas kernels  310 us (95%)
  local copies, waits for them, and re-layouts  14.4 us (4%)
    pallas_call x1, Pallas kernels, shards(): pl.pallas_call(functools.partial(mixer_kernel, seqs, chs, chunks), out_sh...  310 us
    unnamed x12, local copies, waits for them, and re-layouts  14.4 us

profile of v3, /device:TPU:0, one launch (start us, length us, event | category | flops | bytes accessed | tf_op | source)
XLA Modules:
  0.0 325.5 jit_solution(2056085133467898352)
XLA Ops:
  0.6 310.4 %monarch_mixer.1 = (bf16[48,65536]{1,0:T(8,128)(2,1)}, bf16[48,65536]{1,0:T(8,128)(2,1)}, bf16[48,65536]{1,0:T(8,128)(2,1)}, f32[16,512]{1,0:T(8,128)}) custom-call(bf16[48,65536]{1,0:T(8,128)(2,1)} %x_hbm.1, bf16[48,65536]{1,0:T(8,128)(2,1)} %g_hbm.1, bf16[48,65536]{1,0:T(8,128)(2,1)} %k_hbm.1, bf16[32,1024]{1,0:T(8,128)(2,1)} %right_ref.1, ...), custom_call_target="tpu_custom_call" | custom-call | flops 28991029248 | bytes 37748736 | tf_op jit(solution)/shard_map/monarch_mixer/pallas_call | solution.py:483
  311.1 0.0 copy-start
  311.1 0.0 slice-start
  311.1 6.5 %copy.13 = bf16[48,65536]{1,0:T(8,128)(2,1)} copy(bf16[48,65536]{1,0:T(8,128)(2,1)} %get-tuple-element.8) | data formatting | bytes 12582912
  317.6 0.0 copy-done
  317.6 0.0 slice-start.1
  317.6 3.2 copy.14
  320.8 0.0 slice-done
  320.8 1.4 slice-done.1
  322.2 0.0 copy-start.1
  322.2 2.7 copy.15
  324.9 0.0 copy-done.1
  324.9 0.6 copy.16
  (1 shorter events, 0.0 us)
Async XLA Ops:
  311.1 6.6 %copy-start = (bf16[48,65536]{1,0:T(8,128)(2,1)S(1)}, bf16[48,65536]{1,0:T(8,128)(2,1)}, u32[]{:S(2)}) copy-start(bf16[48,65536]{1,0:T(8,128)(2,1)} %get-tuple-element.9) | copy-start | bytes 18874372
  311.1 9.7 %slice-start = ((s8[6291456]{0:T(1024)(128)(4,1)}), s8[4194304]{0:T(1024)(128)(4,1)S(1)}, s32[]{:S(2)}) async-start(s8[6291456]{0:T(1024)(128)(4,1)} %bitcast), calls=%async_computation | async-start | bytes 8388608
  317.6 4.6 %slice-start.1 = ((s8[6291456]{0:T(1024)(128)(4,1)}), s8[2097152]{0:T(1024)(128)(4,1)S(1)}, s32[]{:S(2)}) async-start(s8[6291456]{0:T(1024)(128)(4,1)} %bitcast), calls=%async_computation.1 | async-start | bytes 4194304
  322.2 2.7 copy-start.1
